TPU v7x, 32 devices: a whole 2x2x4 slice. The times are simulated.
32 devices in a mesh: gz: 4 (over y, core), xy: 8 (over z, x).
Axes of the slice: x: 2, y: 2, z: 4, core: 2. Of those that a mesh axis runs over, the one named last changes fastest.
Arguments:
- hodge: float32 [4, 4, 32, 8192], P(None, None, 'gz', 'xy')
- permeability: float32 [32, 8192], P('gz', 'xy')
- storage: float32 [32, 8192], P('gz', 'xy'), may hold values from 0.5 to 2
- pore_volume: float32 [32, 8192], P('gz', 'xy'), may hold values from 0.5 to 2
- source: float32 [32, 8192], P('gz', 'xy'), may hold values from -60 to 60
- saturation_old: float32 [32, 8192], P('gz', 'xy'), may hold values from 0 to 1
- neighbours: int32 [4, 32, 8192], P(None, 'gz', 'xy'), may hold values from 0 to 168, as said below
- upwind: int32 [8, 4, 32, 8192], P(None, None, 'gz', 'xy'), may hold values 0 or 1
- active: int32 [32, 8192], P('gz', 'xy'), may hold values 0 or 1
Outputs:
- pressure: float32 [32, 8192], P('gz', 'xy')
- saturation: float32 [32, 8192], P('gz', 'xy')
Inputs may be any that keep to these rules, and one draw needn't show every extreme that they name: `neighbours`: every code names an offset that stays within the extended block of the cell and outside its corner regions; it is never the cell itself.
All inputs are finite; a program needn't handle non-finite values. No bound on the sum of `upwind` or of `active` on one device may be relied on, other than what follows from the above.
Results may differ from a plain program's by a relative error of at most 0.0001.
Values sent between devices are 32-bit elements; how exact they have to be, the bound alone decides.
A program may use at most 64 MiB of HBM per device.

v0:
```python
import functools

import jax
import jax.numpy as jnp
from jax import lax
from jax.experimental import pallas as pl
from jax.experimental.pallas import tpu as pltpu
from jax.sharding import PartitionSpec as P

REACH = 6
SPAN = 2 * REACH + 1
ITERS = 4
NSUB = 8
FACES = 4
LANES = 128
EDGE = 2 * REACH
NEVER = 99
MESH = pl.DeviceIdType.MESH
UNROLL = 2


def fraction(sat):
    return sat * sat / (sat * sat + 0.5 * (1.0 - sat) * (1.0 - sat))


def chebyshev():
    sigma = 1.0 / 0.9
    rho = 1.0 / sigma
    pairs = []
    for _ in range(ITERS - 1):
        rho_new = 1.0 / (2.0 * sigma - rho)
        pairs.append((rho_new * rho, 2.0 * rho_new / 0.9))
        rho = rho_new
    return pairs


def take(tile, index):
    return jnp.take_along_axis(tile, index, axis=1, mode="promise_in_bounds")


def kernel(
    nz, nx, tiles,
    hodge_h, perm_h, stor_h, pv_h, src_h, sat_h, near_h, up_h, act_h,
    p_out, s_out,
    hodge, perm, stor, pv, src, sat, code, up, act,
    ext, sides, seam, rcode, gindex, coef, zed, total, nears, speed, grow, gain,
    peak, peaks_z, peaks_x,
    load_sem, send_sem, recv_sem, pz_send, pz_recv, px_send, px_recv,
):
    gz = lax.axis_index("gz")
    xy = lax.axis_index("xy")
    loads = [
        pltpu.make_async_copy(a, b, load_sem.at[i])
        for i, (a, b) in enumerate(
            [(sat_h, sat), (near_h, code), (hodge_h, hodge), (perm_h, perm), (stor_h, stor),
             (src_h, src), (pv_h, pv), (act_h, act), (up_h, up)]
        )
    ]
    for load in loads:
        load.start()

    barrier = pltpu.get_barrier_semaphore()
    for k in range(1, nz):
        pl.semaphore_signal(barrier, inc=1, device_id=(lax.rem(gz + k, nz), xy), device_id_type=MESH)
    for k in range(1, nx):
        pl.semaphore_signal(barrier, inc=1, device_id=(gz, lax.rem(xy + k, nx)), device_id_type=MESH)

    lane = lax.broadcasted_iota(jnp.int32, (8, LANES), 1)
    row = lax.broadcasted_iota(jnp.int32, (8, LANES), 0)

    def cols(t):
        return pl.ds(pl.multiple_of(t * LANES, LANES), LANES)

    def to_seam(t, tile, into):
        u = lane - (EDGE * t + REACH)
        index = jnp.where(u < REACH, u, u + (LANES - EDGE)) & (LANES - 1)
        return jnp.where((u >= 0) & (u < EDGE), take(tile, index), into)

    def from_seam(t):
        inner = jnp.where(lane >= LANES - REACH, lane + (EDGE * t + EDGE + REACH - LANES), LANES - 1)
        return jnp.where(lane < REACH, lane + (EDGE * t + REACH), inner)

    def copy(slot, side):
        source, target, device = (
            (ext.at[slot, :, 8:16, :], ext.at[slot, :, 16:24, :], (gz - 1, xy)),
            (ext.at[slot, :, 8:16, :], ext.at[slot, :, 0:8, :], (gz + 1, xy)),
            (ext.at[slot, tiles, 8:16, :], sides.at[slot, 1], (gz, xy - 1)),
            (ext.at[slot, tiles, 8:16, :], sides.at[slot, 0], (gz, xy + 1)),
        )[side]
        return pltpu.make_async_remote_copy(
            src_ref=source, dst_ref=target,
            send_sem=send_sem.at[slot, side], recv_sem=recv_sem.at[slot, side],
            device_id=device, device_id_type=MESH,
        )

    has = (gz > 0, gz < nz - 1, xy > 0, xy < nx - 1)

    def start(slot):
        for side in (2, 3, 0, 1):
            @pl.when(has[side])
            def _():
                copy(slot, side).start()

    def wait_send(slot):
        for side in range(4):
            @pl.when(has[side])
            def _():
                copy(slot, side).wait_send()

    def wait_recv(slot):
        for side in range(4):
            @pl.when(has[side ^ 1])
            def _():
                copy(slot, side).wait_recv()

    loads[0].wait()

    def first_sat(t, seams):
        value = fraction(sat[:, cols(t)])
        ext[ITERS, t, 8:16, :] = value
        return to_seam(t, value, seams)

    zero = jnp.zeros((8, LANES), jnp.float32)
    ext[ITERS, tiles, 8:16, :] = lax.fori_loop(0, tiles, first_sat, zero, unroll=UNROLL)
    pl.semaphore_wait(barrier, nz + nx - 2)
    start(ITERS)

    for load in loads[1:6]:
        load.wait()

    def setup(t, seams):
        weights = []
        for g in range(FACES):
            summed = hodge[0, g, :, cols(t)]
            for f in range(1, FACES):
                summed = summed + hodge[f, g, :, cols(t)]
            weights.append(perm[:, cols(t)] * summed)
        diag = stor[:, cols(t)] + (weights[0] + weights[1] + weights[2] + weights[3])
        for g in range(FACES):
            coef[g, t] = weights[g] / diag
        first = src[:, cols(t)] / diag
        zed[t] = first
        total[t] = first
        ext[0, t, 8:16, :] = first
        return to_seam(t, first, seams)

    ext[0, tiles, 8:16, :] = lax.fori_loop(0, tiles, setup, zero, unroll=UNROLL)
    start(0)

    def rows_code(value):
        return (value * 79) >> 10

    def outside(rc):
        at = row + rc - REACH
        return ((gz == 0) & (at < 0)) | ((gz == nz - 1) & (at >= 8))

    def codes(t, seams):
        grown = []
        for f in range(FACES):
            value = code[f, :, cols(t)]
            rc = rows_code(value)
            col = lane + (value - SPAN * rc - REACH)
            cross = (col < 0) | (col >= LANES)
            gindex[f, t] = col & (LANES - 1)
            rcode[f, t] = jnp.where(cross | outside(rc), NEVER, rc)
            grown.append(to_seam(t, value, seams[f]))
        return tuple(grown)

    seam_codes = lax.fori_loop(0, tiles, codes, (jnp.zeros((8, LANES), jnp.int32),) * FACES)
    for f in range(FACES):
        value = seam_codes[f]
        rc = rows_code(value)
        shift = value - SPAN * rc - REACH
        base = EDGE * ((lane * 43) >> 9)
        here = lane - base
        there = here + shift
        cross = jnp.where(here < REACH, there - REACH, REACH - 1 - there) >= 0
        ours = (lane >= REACH) & (lane < EDGE * tiles + REACH)
        inside = jnp.logical_not(
            ((xy == 0) & (base == 0) & (there < REACH))
            | ((xy == nx - 1) & (base == EDGE * tiles) & (there >= REACH))
        )
        gindex[f, tiles] = (lane + shift) & (LANES - 1)
        rcode[f, tiles] = jnp.where(cross & ours & inside & jnp.logical_not(outside(rc)), rc, NEVER)

    def look(load, t, begin):
        out = list(begin)
        index = [gindex[f, t] for f in range(FACES)]
        rows = [rcode[f, t] for f in range(FACES)]
        for s in range(SPAN):
            x = load(s)
            for f in range(FACES):
                out[f] = jnp.where(rows[f] == s, take(x, index[f]), out[f])
        return out

    def seam_look(slot):
        seam[0:8, :] = ext[slot, tiles, 0:8, :]
        seam[16:24, :] = ext[slot, tiles, 16:24, :]
        left = take(sides[slot, 0], (lane + EDGE * tiles) & (LANES - 1))
        right = take(sides[slot, 1], (lane - EDGE * tiles) & (LANES - 1))
        own = ext[slot, tiles, 8:16, :]
        own = jnp.where(lane < REACH, left, own)
        own = jnp.where(lane >= EDGE * tiles + REACH, right, own)
        seam[8:16, :] = own
        return look(lambda s: seam[2 + s : 10 + s, :], tiles, [zero] * FACES)

    def tile_look(slot, t, seams):
        spread = from_seam(t)
        return look(lambda s: ext[slot, t, 2 + s : 10 + s, :], t, [take(e, spread) for e in seams])

    pairs = chebyshev()
    for step in range(ITERS):
        wait_recv(step)
        seams = seam_look(step)

        if step < ITERS - 1:
            keep, add = pairs[step]

            def advance(t, grown):
                near = tile_look(step, t, seams)
                direction = ext[step, t, 8:16, :]
                z = zed[t] - direction
                for f in range(FACES):
                    z = z + coef[f, t] * near[f]
                    nears[f, t] = near[f] if step == 0 else nears[f, t] + near[f]
                zed[t] = z
                direction = keep * direction + add * z
                total[t] = total[t] + direction
                ext[step + 1, t, 8:16, :] = direction
                return to_seam(t, direction, grown)

            ext[step + 1, tiles, 8:16, :] = lax.fori_loop(0, tiles, advance, zero, unroll=UNROLL)
            start(step + 1)
            wait_send(step)
        else:
            loads[6].wait()

            def finish(t, top):
                near = tile_look(step, t, seams)
                value = total[t]
                p_out[:, cols(t)] = value
                drop = [value - (nears[f, t] + near[f]) for f in range(FACES)]
                rate = zero
                for f in range(FACES):
                    flux = hodge[f, 0, :, cols(t)] * drop[0]
                    for g in range(1, FACES):
                        flux = flux + hodge[f, g, :, cols(t)] * drop[g]
                    fast = jnp.abs(perm[:, cols(t)] * flux)
                    speed[f, t] = fast
                    rate = rate + fast
                return jnp.maximum(top, rate / pv[:, cols(t)])

            peak[0] = lax.fori_loop(0, tiles, finish, zero, unroll=UNROLL)

    def z_copy(k):
        return pltpu.make_async_remote_copy(
            src_ref=peak.at[0], dst_ref=peaks_z.at[k - 1],
            send_sem=pz_send.at[k - 1], recv_sem=pz_recv.at[k - 1],
            device_id=(lax.rem(gz + k, nz), xy), device_id_type=MESH,
        )

    def x_copy(k):
        return pltpu.make_async_remote_copy(
            src_ref=peak.at[1], dst_ref=peaks_x.at[k - 1],
            send_sem=px_send.at[k - 1], recv_sem=px_recv.at[k - 1],
            device_id=(gz, lax.rem(xy + k, nx)), device_id_type=MESH,
        )

    for k in range(1, nz):
        z_copy(k).start()
    loads[7].wait()
    loads[8].wait()
    for k in range(1, nz):
        z_copy(k).wait_recv()
    top = peak[0]
    for k in range(1, nz):
        top = jnp.maximum(top, peaks_z[k - 1])
    peak[1] = top
    for k in range(1, nx):
        x_copy(k).start()

    def inflow(n, t, seams):
        near = tile_look(ITERS + n, t, seams)
        here = -ext[ITERS + n, t, 8:16, :]
        gained = zero
        for f in range(FACES):
            gained = gained + speed[f, t] * jnp.where(up[n, f, :, cols(t)] != 0, near[f], here)
        return gained

    wait_recv(ITERS)
    seams0 = seam_look(ITERS)

    def first_inflow(t, carry):
        grow[t] = inflow(0, t, seams0)
        return carry

    lax.fori_loop(0, tiles, first_inflow, 0, unroll=UNROLL)

    for k in range(1, nx):
        x_copy(k).wait_recv()
    for k in range(1, nx):
        top = jnp.maximum(top, peaks_x[k - 1])
    top = jnp.max(jnp.max(top, axis=1, keepdims=True), axis=0, keepdims=True)
    tau = jnp.broadcast_to(0.8 / top, (8, LANES))

    def first_step(t, grown):
        scale = act[:, cols(t)].astype(jnp.float32) * tau / pv[:, cols(t)]
        gain[t] = scale
        value = sat[:, cols(t)] + scale * grow[t]
        sat[:, cols(t)] = value
        value = fraction(value)
        ext[ITERS + 1, t, 8:16, :] = value
        return to_seam(t, value, grown)

    ext[ITERS + 1, tiles, 8:16, :] = lax.fori_loop(0, tiles, first_step, zero, unroll=UNROLL)
    start(ITERS + 1)
    wait_send(ITERS - 1)
    wait_send(ITERS)
    for k in range(1, nz):
        z_copy(k).wait_send()
    for k in range(1, nx):
        x_copy(k).wait_send()

    for n in range(1, NSUB):
        slot = ITERS + n
        wait_recv(slot)
        seams = seam_look(slot)
        if n < NSUB - 1:
            def substep(t, grown):
                value = sat[:, cols(t)] + gain[t] * inflow(n, t, seams)
                sat[:, cols(t)] = value
                value = fraction(value)
                ext[slot + 1, t, 8:16, :] = value
                return to_seam(t, value, grown)

            ext[slot + 1, tiles, 8:16, :] = lax.fori_loop(0, tiles, substep, zero, unroll=UNROLL)
            start(slot + 1)
        else:
            def last(t, carry):
                s_out[:, cols(t)] = sat[:, cols(t)] + gain[t] * inflow(n, t, seams)
                return carry

            lax.fori_loop(0, tiles, last, 0, unroll=UNROLL)
        wait_send(slot)


def per_device(nz, nx, *args):
    rows, columns = args[1].shape
    tiles = columns // LANES
    slots = ITERS + NSUB
    f32, i32 = jnp.float32, jnp.int32
    scratch = [pltpu.VMEM(a.shape, a.dtype) for a in args]
    plain = (tiles, rows, LANES)
    faces = (FACES, tiles, rows, LANES)
    scratch += [
        pltpu.VMEM((slots, tiles + 1, 3 * rows, LANES), f32),
        pltpu.VMEM((slots, 2, rows, LANES), f32),
        pltpu.VMEM((3 * rows, LANES), f32),
        pltpu.VMEM((FACES, tiles + 1, rows, LANES), i32),
        pltpu.VMEM((FACES, tiles + 1, rows, LANES), i32),
        pltpu.VMEM(faces, f32),
        pltpu.VMEM(plain, f32),
        pltpu.VMEM(plain, f32),
        pltpu.VMEM(faces, f32),
        pltpu.VMEM(faces, f32),
        pltpu.VMEM(plain, f32),
        pltpu.VMEM(plain, f32),
        pltpu.VMEM((2, rows, LANES), f32),
        pltpu.VMEM((nz - 1, rows, LANES), f32),
        pltpu.VMEM((nx - 1, rows, LANES), f32),
        pltpu.SemaphoreType.DMA((len(args),)),
        pltpu.SemaphoreType.DMA((slots, 4)),
        pltpu.SemaphoreType.DMA((slots, 4)),
        pltpu.SemaphoreType.DMA((nz - 1,)),
        pltpu.SemaphoreType.DMA((nz - 1,)),
        pltpu.SemaphoreType.DMA((nx - 1,)),
        pltpu.SemaphoreType.DMA((nx - 1,)),
    ]
    block = jax.ShapeDtypeStruct((rows, columns), f32)
    return tuple(
        pl.pallas_call(
            functools.partial(kernel, nz, nx, tiles),
            out_shape=(block, block),
            in_specs=[pl.BlockSpec(memory_space=pl.ANY)] * len(args),
            out_specs=(pl.BlockSpec(memory_space=pltpu.VMEM),) * 2,
            scratch_shapes=scratch,
            compiler_params=pltpu.CompilerParams(
                collective_id=0, has_side_effects=True, vmem_limit_bytes=32 * 1024 * 1024
            ),
        )(*args)
    )


def solution(mesh):
    placed = (
        P(None, None, "gz", "xy"),
        P("gz", "xy"),
        P("gz", "xy"),
        P("gz", "xy"),
        P("gz", "xy"),
        P("gz", "xy"),
        P(None, "gz", "xy"),
        P(None, None, "gz", "xy"),
        P("gz", "xy"),
    )
    return jax.shard_map(
        functools.partial(per_device, mesh.shape["gz"], mesh.shape["xy"]),
        mesh=mesh,
        in_specs=placed,
        out_specs=(P("gz", "xy"), P("gz", "xy")),
        check_vma=False,
    )
```

profile of v0, /device:TPU:0, one launch (start us, length us, event | category | flops | bytes accessed | tf_op | source)
XLA Modules:
  0.0 81.1 jit_solution(9171252740587425563)
XLA Ops:
  0.6 0.0 copy-start
  0.6 1.2 %copy-done = s32[8,4,8,1024]{3,2,1,0:T(8,128)S(1)} copy-done((s32[8,4,8,1024]{3,2,1,0:T(8,128)S(1)}, s32[8,4,8,1024]{3,2,1,0:T(8,128)}, u32[]{:S(2)}) %copy-start) | copy-done | bytes 1048600
  1.9 0.0 copy-start.1
  1.9 1.0 %copy-done.1 = f32[4,4,8,1024]{3,2,1,0:T(8,128)S(1)} copy-done((f32[4,4,8,1024]{3,2,1,0:T(8,128)S(1)}, f32[4,4,8,1024]{3,2,1,0:T(8,128)}, u32[]{:S(2)}) %copy-start.1) | copy-done | bytes 524312
  2.9 0.0 copy-start.2
  2.9 0.9 %copy-done.2 = s32[4,8,1024]{2,1,0:T(8,128)S(1)} copy-done((s32[4,8,1024]{2,1,0:T(8,128)S(1)}, s32[4,8,1024]{2,1,0:T(8,128)}, u32[]{:S(2)}) %copy-start.2) | copy-done | bytes 131096
  3.8 0.0 copy-start.3
  3.8 0.8 copy-done.3
  4.6 0.0 copy-start.4
  4.6 0.8 copy-done.4
  5.3 0.0 copy-start.5
  5.3 0.8 copy-done.5
  6.1 0.0 copy-start.6
  6.1 0.8 copy-done.6
  6.8 0.0 copy-start.7
  6.8 0.8 copy-done.7
  7.6 0.0 copy-start.8
  7.6 0.8 copy-done.8
  8.4 71.5 %shard_map.104 = (f32[8,1024]{1,0:T(8,128)S(1)}, f32[8,1024]{1,0:T(8,128)S(1)}) custom-call(f32[4,4,8,1024]{3,2,1,0:T(8,128)S(1)} %copy-done.1, f32[8,1024]{1,0:T(8,128)S(1)} %copy-done.3, f32[8,1024]{1,0:T(8,128)S(1)} %copy-done.4, f32[8,1024]{1,0:T(8,128)S(1)} %copy-done.5, f32[8,1024]{1,0:T(8,128)S(1)} %copy-done.6, f32[8,1024]{1,0:T(8,128)S(1)} %copy-done.7, ...), custom_call_target="tpu_custom_call" | custom-call | tf_op jit(solution)/shard_map/pallas_call | solution.py:381
  79.8 0.6 copy.13
  80.5 0.6 copy.14
Async XLA Ops:
  0.6 1.2 %copy-start = (s32[8,4,8,1024]{3,2,1,0:T(8,128)S(1)}, s32[8,4,8,1024]{3,2,1,0:T(8,128)}, u32[]{:S(2)}) copy-start(s32[8,4,8,1024]{3,2,1,0:T(8,128)} %up_h.1) | copy-start | bytes 3145732
  1.9 1.0 %copy-start.1 = (f32[4,4,8,1024]{3,2,1,0:T(8,128)S(1)}, f32[4,4,8,1024]{3,2,1,0:T(8,128)}, u32[]{:S(2)}) copy-start(f32[4,4,8,1024]{3,2,1,0:T(8,128)} %hodge_h.1) | copy-start | bytes 1572868
  2.9 0.9 %copy-start.2 = (s32[4,8,1024]{2,1,0:T(8,128)S(1)}, s32[4,8,1024]{2,1,0:T(8,128)}, u32[]{:S(2)}) copy-start(s32[4,8,1024]{2,1,0:T(8,128)} %near_h.1) | copy-start | bytes 393220
  3.8 0.8 copy-start.3
  4.6 0.8 copy-start.4
  5.3 0.8 copy-start.5
  6.1 0.8 copy-start.6
  6.8 0.8 copy-start.7
  7.6 0.8 copy-start.8
where the time goes:
time: 81.7 us; the launch traced here: 81.1 us
  Pallas kernels  71.5 us (88%)
  local copies, waits for them, and re-layouts  8.94 us (11%)
    pallas_call x1, Pallas kernels, per_device(): pl.pallas_call(functools.partial(kernel, nz, nx, tiles), out_shape=(block...  71.5 us
    unnamed x20, local copies, waits for them, and re-layouts  8.94 us

commit v1 on v0

v1 whole, which is shorter than its diff:
```python
import functools

import jax
import jax.numpy as jnp
from jax import lax
from jax.experimental import pallas as pl
from jax.experimental.pallas import tpu as pltpu
from jax.sharding import PartitionSpec as P

REACH = 6
SPAN = 2 * REACH + 1
ITERS = 4
NSUB = 8
FACES = 4
LANES = 128
EDGE = 2 * REACH
NEVER = 99
MESH = pl.DeviceIdType.MESH
SENT = ITERS + NSUB
SAT = ITERS
GAIN = ITERS + 1
FRAC0 = SENT
FRAC1 = SENT + 1


def fraction(sat):
    return sat * sat / (sat * sat + 0.5 * (1.0 - sat) * (1.0 - sat))


def chebyshev():
    sigma = 1.0 / 0.9
    rho = 1.0 / sigma
    pairs = []
    for _ in range(ITERS - 1):
        rho_new = 1.0 / (2.0 * sigma - rho)
        pairs.append((rho_new * rho, 2.0 * rho_new / 0.9))
        rho = rho_new
    return pairs


def take(tile, index):
    return jnp.take_along_axis(tile, index, axis=1, mode="promise_in_bounds")


def kernel(
    nz, nx, tiles,
    hodge_h, perm_h, stor_h, pv_h, src_h, sat_h, near_h, up_h, act_h,
    p_out, s_out,
    hodge, perm, stor, pv, src, sat, code, up, act,
    own, halo, sides, outer, rcode, gindex, coef, zed, total, nears, near0, speed, acc, gain,
    peak, peaks_z, peaks_x,
    load_sem, send_sem, recv_sem, pz_send, pz_recv, px_send, px_recv,
):
    gz = lax.axis_index("gz")
    xy = lax.axis_index("xy")
    loads = [
        pltpu.make_async_copy(a, b, load_sem.at[i])
        for i, (a, b) in enumerate(
            [(sat_h, sat), (near_h, code), (hodge_h, hodge), (perm_h, perm), (stor_h, stor),
             (src_h, src), (pv_h, pv), (act_h, act), (up_h, up)]
        )
    ]
    for load in loads:
        load.start()

    barrier = pltpu.get_barrier_semaphore()
    for k in range(1, nz):
        pl.semaphore_signal(barrier, inc=1, device_id=(lax.rem(gz + k, nz), xy), device_id_type=MESH)
    for k in range(1, nx):
        pl.semaphore_signal(barrier, inc=1, device_id=(gz, lax.rem(xy + k, nx)), device_id_type=MESH)

    lane = lax.broadcasted_iota(jnp.int32, (8, LANES), 1)
    row = lax.broadcasted_iota(jnp.int32, (8, LANES), 0)

    def cols(t):
        return pl.ds(pl.multiple_of(t * LANES, LANES), LANES)

    def to_seam(t, tile, into):
        u = lane - (EDGE * t + REACH)
        index = jnp.where(u < REACH, u, u + (LANES - EDGE)) & (LANES - 1)
        return jnp.where((u >= 0) & (u < EDGE), take(tile, index), into)

    def from_seam(t):
        inner = jnp.where(lane >= LANES - REACH, lane + (EDGE * t + EDGE + REACH - LANES), LANES - 1)
        return jnp.where(lane < REACH, lane + (EDGE * t + REACH), inner)

    def copy(slot, side):
        source, target, device = (
            (own.at[slot, :, 0:8, :], halo.at[slot, :, 8:16, :], (gz - 1, xy)),
            (own.at[slot, :, 0:8, :], halo.at[slot, :, 0:8, :], (gz + 1, xy)),
            (own.at[slot, tiles, 0:8, :], sides.at[slot, 1], (gz, xy - 1)),
            (own.at[slot, tiles, 0:8, :], sides.at[slot, 0], (gz, xy + 1)),
        )[side]
        return pltpu.make_async_remote_copy(
            src_ref=source, dst_ref=target,
            send_sem=send_sem.at[slot, side], recv_sem=recv_sem.at[slot, side],
            device_id=device, device_id_type=MESH,
        )

    has = (gz > 0, gz < nz - 1, xy > 0, xy < nx - 1)

    def start(slot):
        for side in (2, 3, 0, 1):
            @pl.when(has[side])
            def _():
                copy(slot, side).start()

    def wait_send(slot):
        for side in range(4):
            @pl.when(has[side])
            def _():
                copy(slot, side).wait_send()

    def wait_recv(slot, across):
        for side in (2, 3) if across else (0, 1):
            @pl.when(has[side ^ 1])
            def _():
                copy(slot, side).wait_recv()

    zero = jnp.zeros((8, LANES), jnp.float32)

    def over(body, begin, first=0, last=tiles):
        return lax.fori_loop(first, last, body, begin, unroll=last - first)

    def put(slot, t, value):
        own[slot, t, 0:8, :] = value
        own[slot, t, 8:16, :] = value

    loads[0].wait()

    def first_sat(t, seams):
        value = sat[:, cols(t)]
        put(SAT, t, value)
        put(FRAC0, t, fraction(value))
        return to_seam(t, value, seams)

    value = over(first_sat, zero)
    put(SAT, tiles, value)
    put(FRAC0, tiles, fraction(value))
    pl.semaphore_wait(barrier, nz + nx - 2)

    for load in loads[1:6]:
        load.wait()

    def setup(t, seams):
        weights = []
        for g in range(FACES):
            summed = hodge[0, g, :, cols(t)]
            for f in range(1, FACES):
                summed = summed + hodge[f, g, :, cols(t)]
            weights.append(perm[:, cols(t)] * summed)
        diag = stor[:, cols(t)] + (weights[0] + weights[1] + weights[2] + weights[3])
        for g in range(FACES):
            coef[g, t] = weights[g] / diag
        first = src[:, cols(t)] / diag
        zed[t] = first
        total[t] = first
        put(0, t, first)
        return to_seam(t, first, seams)

    put(0, tiles, over(setup, zero))
    start(0)
    start(SAT)

    def rows_code(value):
        return (value * 79) >> 10

    def outside(rc):
        at = row + rc - REACH
        return ((gz == 0) & (at < 0)) | ((gz == nz - 1) & (at >= 8))

    def key(rc):
        at = row + rc - REACH
        turn = (rc - REACH) & 7
        return jnp.where((at >= 0) & (at < 8), turn, turn + 8)

    def codes(t, seams):
        grown = []
        for f in range(FACES):
            value = code[f, :, cols(t)]
            rc = rows_code(value)
            col = lane + (value - SPAN * rc - REACH)
            cross = (col < 0) | (col >= LANES)
            gindex[f, t] = col & (LANES - 1)
            rcode[f, t] = jnp.where(cross | outside(rc), NEVER, key(rc))
            grown.append(to_seam(t, value, seams[f]))
        return tuple(grown)

    seam_codes = lax.fori_loop(0, tiles, codes, (jnp.zeros((8, LANES), jnp.int32),) * FACES)
    for f in range(FACES):
        value = seam_codes[f]
        rc = rows_code(value)
        shift = value - SPAN * rc - REACH
        base = EDGE * ((lane * 43) >> 9)
        here = lane - base
        there = here + shift
        cross = jnp.where(here < REACH, there - REACH, REACH - 1 - there) >= 0
        ours = (lane >= REACH) & (lane < EDGE * tiles + REACH)
        left = (base == 0) & (there < REACH)
        right = (base == EDGE * tiles) & (there >= REACH)
        inside = jnp.logical_not(((xy == 0) & left) | ((xy == nx - 1) & right))
        rows = jnp.where(left | right, key(rc) + 16, key(rc))
        gindex[f, tiles] = (lane + shift) & (LANES - 1)
        rcode[f, tiles] = jnp.where(cross & ours & inside & jnp.logical_not(outside(rc)), rows, NEVER)

    def look(load, t, begin, first, last):
        out = list(begin)
        index = [gindex[f, t] for f in range(FACES)]
        rows = [rcode[f, t] for f in range(FACES)]
        for s in range(first, last):
            x = load(s & 7)
            for f in range(FACES):
                out[f] = jnp.where(rows[f] == s, take(x, index[f]), out[f])
        return out

    def look_here(slot):
        def body(t, carry):
            near = look(lambda q: own[slot, t, pl.ds(q, 8), :], t, [zero] * FACES, 0, 8)
            for f in range(FACES):
                acc[f, t] = near[f]
            return carry

        over(body, 0, 0, tiles + 1)

    def look_rows(slot, t):
        return look(
            lambda q: halo[slot, t, pl.ds(q, 8), :], t, [acc[f, t] for f in range(FACES)], 9, 16
        )

    def spread(seams, t):
        index = from_seam(t)
        return [take(e, index) for e in seams]

    def look_sides(seams, left, right):
        value = jnp.where(
            lane < REACH,
            take(left, (lane + EDGE * tiles) & (LANES - 1)),
            take(right, (lane - EDGE * tiles) & (LANES - 1)),
        )
        outer[0:8, :] = value
        outer[8:16, :] = value
        return look(lambda q: outer[pl.ds(q, 8), :], tiles, seams, 16, 24)

    def near_step(slot, arrive, finish, begin, while_waiting=None):
        look_here(slot)
        if while_waiting is not None:
            while_waiting()
        arrive(False)
        seams = look_rows(slot, tiles)

        def body(t, carry):
            rows = look_rows(slot, t)
            near = [a + b for a, b in zip(rows, spread(seams, t))]
            return finish(t, near, carry)

        carry = over(body, begin, 1, tiles - 1)
        ends = [(t, look_rows(slot, t)) for t in (0, tiles - 1)]
        left, right = arrive(True)
        seams = look_sides(seams, left, right)
        for t, rows in ends:
            near = [a + b for a, b in zip(rows, spread(seams, t))]
            carry = finish(t, near, carry)
        return carry

    def arrived(slot):
        def arrive(across):
            wait_recv(slot, across)
            return (sides[slot, 0], sides[slot, 1]) if across else None

        return arrive

    def arrive_first(across):
        wait_recv(SAT, across)
        if across:
            return fraction(sides[SAT, 0]), fraction(sides[SAT, 1])

        def body(t, carry):
            halo[FRAC0, t] = fraction(halo[SAT, t])
            return carry

        over(body, 0, 0, tiles + 1)

    def first_near():
        def finish(t, near, carry):
            for f in range(FACES):
                near0[f, t] = near[f]
            return carry

        near_step(FRAC0, arrive_first, finish, 0)

    pairs = chebyshev()
    for step in range(ITERS):
        if step < ITERS - 1:
            keep, add = pairs[step]

            def advance(t, near, grown):
                direction = own[step, t, 0:8, :]
                z = zed[t] - direction
                for f in range(FACES):
                    z = z + coef[f, t] * near[f]
                    nears[f, t] = near[f] if step == 0 else nears[f, t] + near[f]
                zed[t] = z
                direction = keep * direction + add * z
                total[t] = total[t] + direction
                put(step + 1, t, direction)
                return to_seam(t, direction, grown)

            put(step + 1, tiles, near_step(step, arrived(step), advance, zero))
            start(step + 1)
            wait_send(step)
            if step == 0:
                first_near()
        else:
            loads[6].wait()

            def flow(t, near, top):
                value = total[t]
                p_out[:, cols(t)] = value
                drop = [value - (nears[f, t] + near[f]) for f in range(FACES)]
                rate = zero
                for f in range(FACES):
                    flux = hodge[f, 0, :, cols(t)] * drop[0]
                    for g in range(1, FACES):
                        flux = flux + hodge[f, g, :, cols(t)] * drop[g]
                    fast = jnp.abs(perm[:, cols(t)] * flux)
                    speed[f, t] = fast
                    rate = rate + fast
                return jnp.maximum(top, rate / pv[:, cols(t)])

            peak[0] = near_step(step, arrived(step), flow, zero)

    def z_copy(k):
        return pltpu.make_async_remote_copy(
            src_ref=peak.at[0], dst_ref=peaks_z.at[k - 1],
            send_sem=pz_send.at[k - 1], recv_sem=pz_recv.at[k - 1],
            device_id=(lax.rem(gz + k, nz), xy), device_id_type=MESH,
        )

    def x_copy(k):
        return pltpu.make_async_remote_copy(
            src_ref=peak.at[1], dst_ref=peaks_x.at[k - 1],
            send_sem=px_send.at[k - 1], recv_sem=px_recv.at[k - 1],
            device_id=(gz, lax.rem(xy + k, nx)), device_id_type=MESH,
        )

    for k in range(1, nz):
        z_copy(k).start()
    loads[7].wait()
    loads[8].wait()

    def inflow(n, slot, t, near):
        here = -own[slot, t, 0:8, :]
        gained = zero
        for f in range(FACES):
            gained = gained + speed[f, t] * jnp.where(up[n, f, :, cols(t)] != 0, near[f], here)
        return gained

    def first_gain(t, grown):
        scale = act[:, cols(t)].astype(jnp.float32) / pv[:, cols(t)]
        gain[t] = scale
        value = scale * inflow(0, FRAC0, t, [near0[f, t] for f in range(FACES)])
        put(GAIN, t, value)
        return to_seam(t, value, grown)

    put(GAIN, tiles, over(first_gain, zero))
    start(GAIN)
    for k in range(1, nz):
        z_copy(k).wait_recv()
    top = peak[0]
    for k in range(1, nz):
        top = jnp.maximum(top, peaks_z[k - 1])
    peak[1] = top
    for k in range(1, nx):
        x_copy(k).start()
    wait_send(ITERS - 1)
    wait_send(SAT)
    for k in range(1, nz):
        z_copy(k).wait_send()
    for k in range(1, nx):
        x_copy(k).wait_recv()
    for k in range(1, nx):
        top = jnp.maximum(top, peaks_x[k - 1])
    top = jnp.max(jnp.max(top, axis=1, keepdims=True), axis=0, keepdims=True)
    tau = jnp.broadcast_to(0.8 / top, (8, LANES))

    def first_step(t, carry):
        gain[t] = gain[t] * tau
        value = sat[:, cols(t)] + tau * own[GAIN, t, 0:8, :]
        sat[:, cols(t)] = value
        put(FRAC1, t, fraction(value))
        return carry

    over(first_step, 0)
    put(FRAC1, tiles, fraction(own[SAT, tiles, 0:8, :] + tau * own[GAIN, tiles, 0:8, :]))

    def arrive_second(across):
        wait_recv(GAIN, across)
        if across:
            return tuple(fraction(sides[SAT, i] + tau * sides[GAIN, i]) for i in range(2))

        def body(t, carry):
            for part in (slice(0, 8), slice(8, 16)):
                halo[FRAC1, t, part, :] = fraction(halo[SAT, t, part, :] + tau * halo[GAIN, t, part, :])
            return carry

        over(body, 0, 0, tiles + 1)

    for n in range(1, NSUB):
        slot = FRAC1 if n == 1 else ITERS + n
        arrive = arrive_second if n == 1 else arrived(slot)
        if n < NSUB - 1:
            def substep(t, near, grown):
                value = sat[:, cols(t)] + gain[t] * inflow(n, slot, t, near)
                sat[:, cols(t)] = value
                value = fraction(value)
                put(ITERS + n + 1, t, value)
                return to_seam(t, value, grown)

            put(ITERS + n + 1, tiles, near_step(slot, arrive, substep, zero))
            start(ITERS + n + 1)
        else:
            def last(t, near, carry):
                s_out[:, cols(t)] = sat[:, cols(t)] + gain[t] * inflow(n, slot, t, near)
                return carry

            near_step(slot, arrive, last, 0)
        wait_send(GAIN if n == 1 else slot)
    for k in range(1, nx):
        x_copy(k).wait_send()


def per_device(nz, nx, *args):
    rows, columns = args[1].shape
    tiles = columns // LANES
    slots = SENT + 2
    f32, i32 = jnp.float32, jnp.int32
    scratch = [pltpu.VMEM(a.shape, a.dtype) for a in args]
    plain = (tiles, rows, LANES)
    faces = (FACES, tiles, rows, LANES)
    scratch += [
        pltpu.VMEM((slots, tiles + 1, 2 * rows, LANES), f32),
        pltpu.VMEM((slots, tiles + 1, 2 * rows, LANES), f32),
        pltpu.VMEM((SENT, 2, rows, LANES), f32),
        pltpu.VMEM((2 * rows, LANES), f32),
        pltpu.VMEM((FACES, tiles + 1, rows, LANES), i32),
        pltpu.VMEM((FACES, tiles + 1, rows, LANES), i32),
        pltpu.VMEM(faces, f32),
        pltpu.VMEM(plain, f32),
        pltpu.VMEM(plain, f32),
        pltpu.VMEM(faces, f32),
        pltpu.VMEM(faces, f32),
        pltpu.VMEM(faces, f32),
        pltpu.VMEM((FACES, tiles + 1, rows, LANES), f32),
        pltpu.VMEM(plain, f32),
        pltpu.VMEM((2, rows, LANES), f32),
        pltpu.VMEM((nz - 1, rows, LANES), f32),
        pltpu.VMEM((nx - 1, rows, LANES), f32),
        pltpu.SemaphoreType.DMA((len(args),)),
        pltpu.SemaphoreType.DMA((SENT, 4)),
        pltpu.SemaphoreType.DMA((SENT, 4)),
        pltpu.SemaphoreType.DMA((nz - 1,)),
        pltpu.SemaphoreType.DMA((nz - 1,)),
        pltpu.SemaphoreType.DMA((nx - 1,)),
        pltpu.SemaphoreType.DMA((nx - 1,)),
    ]
    block = jax.ShapeDtypeStruct((rows, columns), f32)
    return tuple(
        pl.pallas_call(
            functools.partial(kernel, nz, nx, tiles),
            out_shape=(block, block),
            in_specs=[pl.BlockSpec(memory_space=pl.ANY)] * len(args),
            out_specs=(pl.BlockSpec(memory_space=pltpu.VMEM),) * 2,
            scratch_shapes=scratch,
            compiler_params=pltpu.CompilerParams(
                collective_id=0, has_side_effects=True, vmem_limit_bytes=60 * 1024 * 1024
            ),
        )(*args)
    )


def solution(mesh):
    placed = (
        P(None, None, "gz", "xy"),
        P("gz", "xy"),
        P("gz", "xy"),
        P("gz", "xy"),
        P("gz", "xy"),
        P("gz", "xy"),
        P(None, "gz", "xy"),
        P(None, None, "gz", "xy"),
        P("gz", "xy"),
    )
    return jax.shard_map(
        functools.partial(per_device, mesh.shape["gz"], mesh.shape["xy"]),
        mesh=mesh,
        in_specs=placed,
        out_specs=(P("gz", "xy"), P("gz", "xy")),
        check_vma=False,
    )
```

time: 81.7 us -> 57.7 us (0.71)
  Pallas kernels: 71.5 us -> 54 us
  local copies, waits for them, and re-layouts: 8.94 us -> 2 us
    pallas_call x1, Pallas kernels: 71.5 us -> 54 us  [per_device(): pl.pallas_call(functools.partial(kernel, nz, nx, tiles), out_shape=(block...]
    unnamed x20 -> x4, local copies, waits for them, and re-layouts: 8.94 us -> 2 us
where the time goes in v1:
time: 57.7 us; the launch traced here: 56.6 us
  Pallas kernels  54 us (94%)
  local copies, waits for them, and re-layouts  2 us (3%)
  between operations  0.65 us (1%)
    pallas_call x1, Pallas kernels, per_device(): pl.pallas_call(functools.partial(kernel, nz, nx, tiles), out_shape=(block...  54 us
    unnamed x4, local copies, waits for them, and re-layouts  2 us

profile of v1, /device:TPU:0, one launch (start us, length us, event | category | flops | bytes accessed | tf_op | source)
XLA Modules:
  0.0 56.6 jit_solution(8425794406826702465)
XLA Ops:
  0.6 54.0 %shard_map.104 = (f32[8,1024]{1,0:T(8,128)}, f32[8,1024]{1,0:T(8,128)}) custom-call(f32[4,4,8,1024]{3,2,1,0:T(8,128)} %hodge_h.1, f32[8,1024]{1,0:T(8,128)} %perm_h.1, f32[8,1024]{1,0:T(8,128)} %stor_h.1, f32[8,1024]{1,0:T(8,128)} %pv_h.1, f32[8,1024]{1,0:T(8,128)} %src_h.1, f32[8,1024]{1,0:T(8,128)} %sat_h.1, s32[4,8,1024]{2,1,0:T(8,128)} %near_h.1, ...), custom_call_target="tpu_custom_call" | custom-call | tf_op jit(solution)/shard_map/pallas_call | solution.py:468
  54.6 0.0 copy-start
  54.6 1.4 %copy.13 = f32[8,1024]{1,0:T(8,128)} copy(f32[8,1024]{1,0:T(8,128)} %get-tuple-element.4) | data formatting | bytes 65536
  56.0 0.0 copy-done
  56.0 0.6 %copy.14 = f32[8,1024]{1,0:T(8,128)} copy(f32[8,1024]{1,0:T(8,128)S(1)} %copy-done) | data formatting | bytes 65536
Async XLA Ops:
  54.6 1.4 %copy-start = (f32[8,1024]{1,0:T(8,128)S(1)}, f32[8,1024]{1,0:T(8,128)}, u32[]{:S(2)}) copy-start(f32[8,1024]{1,0:T(8,128)} %get-tuple-element.5) | copy-start | bytes 98308

commit v2 on v1

--- a/solution.py
+++ b/solution.py
@@ -207,10 +207,9 @@
         out = list(begin)
         index = [gindex[f, t] for f in range(FACES)]
         rows = [rcode[f, t] for f in range(FACES)]
-        for s in range(first, last):
-            x = load(s & 7)
-            for f in range(FACES):
-                out[f] = jnp.where(rows[f] == s, take(x, index[f]), out[f])
+        for f in range(FACES):
+            for s in range(first, last):
+                out[f] = jnp.where(rows[f] == s, take(load(s & 7), index[f]), out[f])
         return out
 
     def look_here(slot):

time: 57.7 us -> 53.6 us (0.929)
  Pallas kernels: 54 us -> 50.1 us
    pallas_call x1, Pallas kernels: 54 us -> 50.1 us  [per_device(): pl.pallas_call(functools.partial(kernel, nz, nx, tiles), out_shape=(block...]
where the time goes in v2:
time: 53.6 us; the launch traced here: 52.7 us
  Pallas kernels  50.1 us (93%)
  local copies, waits for them, and re-layouts  2 us (4%)
  between operations  0.65 us (1%)
    pallas_call x1, Pallas kernels, per_device(): pl.pallas_call(functools.partial(kernel, nz, nx, tiles), out_shape=(block...  50.1 us
    unnamed x4, local copies, waits for them, and re-layouts  2 us

profile of v2, /device:TPU:0, one launch (start us, length us, event | category | flops | bytes accessed | tf_op | source)
XLA Modules:
  0.0 52.7 jit_solution(16212287458834768601)
XLA Ops:
  0.6 50.1 %shard_map.104 = (f32[8,1024]{1,0:T(8,128)}, f32[8,1024]{1,0:T(8,128)}) custom-call(f32[4,4,8,1024]{3,2,1,0:T(8,128)} %hodge_h.1, f32[8,1024]{1,0:T(8,128)} %perm_h.1, f32[8,1024]{1,0:T(8,128)} %stor_h.1, f32[8,1024]{1,0:T(8,128)} %pv_h.1, f32[8,1024]{1,0:T(8,128)} %src_h.1, f32[8,1024]{1,0:T(8,128)} %sat_h.1, s32[4,8,1024]{2,1,0:T(8,128)} %near_h.1, ...), custom_call_target="tpu_custom_call" | custom-call | tf_op jit(solution)/shard_map/pallas_call | solution.py:467
  50.7 0.0 copy-start
  50.7 1.4 %copy.13 = f32[8,1024]{1,0:T(8,128)} copy(f32[8,1024]{1,0:T(8,128)} %get-tuple-element.4) | data formatting | bytes 65536
  52.1 0.0 copy-done
  52.1 0.6 %copy.14 = f32[8,1024]{1,0:T(8,128)} copy(f32[8,1024]{1,0:T(8,128)S(1)} %copy-done) | data formatting | bytes 65536
Async XLA Ops:
  50.7 1.4 %copy-start = (f32[8,1024]{1,0:T(8,128)S(1)}, f32[8,1024]{1,0:T(8,128)}, u32[]{:S(2)}) copy-start(f32[8,1024]{1,0:T(8,128)} %get-tuple-element.5) | copy-start | bytes 98308
